TPU v7x, 32 devices: a whole 2x2x4 slice. The times are simulated.
32 devices in a mesh: col: 4 (over z), row: 8 (over y, x, core).
Axes of the slice: x: 2, y: 2, z: 4, core: 2. Of those that a mesh axis runs over, the one named last changes fastest.
Arguments:
- factor: float32 [8192, 2048], P('row', 'col'), may hold values from -100 to 100
- support: int32 [16, 64], P(None, 'row'), may hold values from 0 to 1, as said below
- plan: int32 [2, 16], replicated, may hold values from 0 to 15, as said below
Outputs:
- rotated_factor: float32 [8192, 2048], P('row', 'col')
Inputs may be any that keep to these rules, and one draw needn't show every extreme that they name: Every column block has at least one row block in its support. `plan`: each row is a permutation; cut each round's row into groups of 4 consecutive positions (group g on index g of col); the 4 blocks of any group sit in 4 different groups of the previous round's row, where the order before round 0 is 0, 1, ..., 15.
All inputs are finite; a program needn't handle non-finite values.
Results may differ from a plain program's by a relative error of at most 0.0003.
Values sent between devices are 32-bit elements; how exact they have to be, the bound alone decides.
A program may use at most 128 MiB of HBM per device.

v0:
```python
import jax
import jax.numpy as jnp
from jax import lax
from jax.sharding import PartitionSpec as P

W = 128
RB = 128
ROUNDS = 2
precise = lax.Precision.HIGHEST
damping = 0.01


def skew_terms(gram_rows, diag_rows, diag_cols):
    spread = diag_rows[:, :, None] - diag_cols[:, None, :]
    joined = diag_rows[:, :, None] + diag_cols[:, None, :]
    return (
        gram_rows * spread / (spread * spread + gram_rows * gram_rows + damping * joined * joined)
    )


def cayley(skew_matrix):
    size_here = skew_matrix.shape[0]
    identity = jnp.eye(size_here, dtype=jnp.float32)
    halved = 0.5 * skew_matrix
    minus_half = identity - halved
    numerator = jnp.dot(minus_half, minus_half, precision=precise)
    definite = identity + jnp.dot(halved.T, halved, precision=precise)
    lower_factor = jnp.linalg.cholesky(definite)
    return jax.scipy.linalg.cho_solve((lower_factor, True), numerator)


def local_gram(left_cols, right_cols):
    return jnp.einsum("rpi,rpj->pij", left_cols, right_cols, precision=precise)


def on_device(factor, support, plan):
    rows_here = factor.shape[0]
    slot_count = factor.shape[1] // W
    group_count = lax.axis_size("col")
    col_place = lax.axis_index("col")
    pair_count = slot_count // 2
    own_support = lax.dynamic_slice_in_dim(support, col_place * slot_count, slot_count, 0)
    row_mask = jnp.repeat(own_support.T, RB, axis=0).astype(jnp.float32)
    current = factor.reshape(rows_here, slot_count, W) * row_mask[:, :, None]
    previous = jnp.arange(slot_count * group_count, dtype=jnp.int32)
    my_slots = col_place * slot_count + jnp.arange(slot_count, dtype=jnp.int32)
    group_ids = jnp.arange(group_count, dtype=jnp.int32)
    for round_index in range(ROUNDS):
        order_now = plan[round_index]
        located = jnp.argsort(previous)[order_now]
        wanted = located[my_slots]
        new_place = jnp.argsort(order_now)[previous[my_slots]]
        send_pick = (new_place[None, :] // slot_count == group_ids[:, None]).astype(jnp.float32)
        outgoing = jnp.einsum("dt,rtw->rdw", send_pick, current, precision=precise)
        incoming = lax.all_to_all(outgoing, "col", split_axis=1, concat_axis=1, tiled=True)
        take_pick = (wanted[:, None] // slot_count == group_ids[None, :]).astype(jnp.float32)
        arranged = jnp.einsum("sd,rdw->rsw", take_pick, incoming, precision=precise)
        paired = arranged.reshape(rows_here, pair_count, 2 * W)
        gram_matrix = lax.psum(local_gram(paired, paired), "row")
        diagonal_terms = jnp.diagonal(gram_matrix, axis1=1, axis2=2)
        skew_matrix = skew_terms(gram_matrix, diagonal_terms, diagonal_terms)
        rotations = jax.vmap(cayley)(skew_matrix)
        rotated = jnp.einsum("rpi,pij->rpj", paired, rotations, precision=precise)
        current = rotated.reshape(rows_here, slot_count, W)
        previous = order_now
    return current.reshape(rows_here, slot_count * W)


def solution(mesh):
    return jax.shard_map(
        on_device,
        mesh=mesh,
        in_specs=(P("row", "col"), P(None, "row"), P()),
        out_specs=P("row", "col"),
        check_vma=False,
    )
```

profile of v0, /device:TPU:0, one launch (start us, length us, event | category | flops | bytes accessed | tf_op | source)
XLA Modules:
  0.0 565.6 jit_solution(1841204664896612224)
XLA Ops:
  20.0 6.4 %all-to-all-start = ((f32[1024,4,128]{2,0,1:T(8,128)}), f32[1024,4,128]{2,0,1:T(8,128)S(1)}, u32[]{:S(2)}, u32[]{:S(2)}) async-start(f32[1024,4,128]{2,0,1:T(8,128)} %copy.118), calls=%async_computation | async-start | bytes 4194304 | tf_op jit(solution)/shard_map/all_to_all | solution.py:55
  29.1 45.5 %all-to-all-done = f32[1024,4,128]{2,0,1:T(8,128)S(1)} async-done(((f32[1024,4,128]{2,0,1:T(8,128)}), f32[1024,4,128]{2,0,1:T(8,128)S(1)}, u32[]{:S(2)}, u32[]{:S(2)}) %all-to-all-start) | async-done | bytes 2097184 | tf_op jit(solution)/shard_map/all_to_all | solution.py:55
  74.6 4.6 fusion.17
  82.6 4.3 fusion.12
  87.0 53.7 %all-reduce.4.cloned.1.call-done = f32[2,256,256]{1,2,0:T(8,128)} async-done(((f32[2,256,256]{1,2,0:T(8,128)}), f32[2,256,256]{1,2,0:T(8,128)}) %all-reduce.4.cloned.1.call-update) | async-done | bytes 524304 | tf_op jit(solution)/shard_map/psum | solution.py:59
  140.7 17.2 %copy.123 = f32[2,256,256]{0,2,1:T(8,128)} copy(f32[2,256,256]{1,2,0:T(8,128)} %all-reduce.4.cloned.1.call-done) | data formatting | bytes 1048576 | tf_op jit(solution)/shard_map/psum | solution.py:59
  162.5 23.5 %custom-call.23 = f32[2,128,128]{2,1,0:T(8,128)S(1)} custom-call(f32[2,128,128]{2,1,0:T(8,128)S(1)} %cholesky.198), custom_call_target="Cholesky" | custom-call | tf_op jit(solution)/shard_map/vmap(jit(cholesky))/cholesky | solution.py:28
  186.1 20.2 %custom-call.24 = f32[2,1,128,128]{2,3,1,0:T(8,128)S(1)} custom-call(f32[2,1,128,128]{3,2,1,0:T(8,128)S(1)} %select_bitcast_fusion.1), custom_call_target="InvertDiagBlocksLowerTriangular" | custom-call | tf_op jit(solution)/shard_map/vmap(jit(cholesky))/cholesky | solution.py:28
  208.8 23.5 %custom-call.25 = f32[2,128,128]{2,1,0:T(8,128)S(1)} custom-call(f32[2,128,128]{2,1,0:T(8,128)S(1)} %convolution_subtract_fusion.5), custom_call_target="Cholesky" | custom-call | tf_op jit(solution)/shard_map/vmap(jit(cholesky))/cholesky | solution.py:28
  232.8 4.1 while.4
  236.9 39.5 %custom-call.26 = f32[2,2,128,128]{2,3,1,0:T(8,128)S(1)} custom-call(f32[2,2,128,128]{3,2,1,0:T(8,128)S(1)} %bitcast.143), custom_call_target="InvertDiagBlocksLowerTriangular" | custom-call | tf_op jit(solution)/shard_map/vmap(jit(_cho_solve))/triangular_solve | solution.py:29
  281.6 4.9 fusion.10
  292.1 4.5 all-to-all-start.1
  298.0 46.2 %all-to-all-done.1 = f32[1024,4,128]{2,0,1:T(8,128)} async-done(((f32[1024,4,128]{2,0,1:T(8,128)}), f32[1024,4,128]{2,0,1:T(8,128)}, u32[]{:S(2)}, u32[]{:S(2)}) %all-to-all-start.1) | async-done | bytes 2097184 | tf_op jit(solution)/shard_map/all_to_all | solution.py:55
  344.1 6.1 %fusion.20 = f32[1024,4,128]{2,1,0:T(4,128)} fusion(f32[1024,4,128]{2,0,1:T(8,128)} %all-to-all-done.1, s32[4]{0:T(128)S(1)} %and_select_fusion), kind=kOutput, calls=%fused_computation.30 | convolution fusion | flops 25165840 | bytes 4194320 | tf_op jit(solution)/shard_map/sd,rdw->rsw/dot_general | solution.py:57
  353.6 4.3 fusion.8
  357.9 52.2 %all-reduce.6.cloned.1.call-done = f32[2,256,256]{1,2,0:T(8,128)} async-done(((f32[2,256,256]{1,2,0:T(8,128)}), f32[2,256,256]{1,2,0:T(8,128)}) %all-reduce.6.cloned.1.call-update) | async-done | bytes 524304 | tf_op jit(solution)/shard_map/psum | solution.py:59
  410.1 17.2 %copy.145 = f32[2,256,256]{0,2,1:T(8,128)} copy(f32[2,256,256]{1,2,0:T(8,128)} %all-reduce.6.cloned.1.call-done) | data formatting | bytes 1048576 | tf_op jit(solution)/shard_map/psum | solution.py:59
  432.0 23.5 %custom-call.27 = f32[2,128,128]{2,1,0:T(8,128)S(1)} custom-call(f32[2,128,128]{2,1,0:T(8,128)S(1)} %cholesky.201), custom_call_target="Cholesky" | custom-call | tf_op jit(solution)/shard_map/vmap(jit(cholesky))/cholesky | solution.py:28
  455.5 20.1 %custom-call.28 = f32[2,1,128,128]{2,3,1,0:T(8,128)S(1)} custom-call(f32[2,1,128,128]{3,2,1,0:T(8,128)S(1)} %select_bitcast_fusion), custom_call_target="InvertDiagBlocksLowerTriangular" | custom-call | tf_op jit(solution)/shard_map/vmap(jit(cholesky))/cholesky | solution.py:28
  478.1 23.5 %custom-call.29 = f32[2,128,128]{2,1,0:T(8,128)S(1)} custom-call(f32[2,128,128]{2,1,0:T(8,128)S(1)} %convolution_subtract_fusion.4), custom_call_target="Cholesky" | custom-call | tf_op jit(solution)/shard_map/vmap(jit(cholesky))/cholesky | solution.py:28
  502.0 4.1 while.5
  506.2 39.5 %custom-call.30 = f32[2,2,128,128]{2,3,1,0:T(8,128)S(1)} custom-call(f32[2,2,128,128]{3,2,1,0:T(8,128)S(1)} %bitcast.142), custom_call_target="InvertDiagBlocksLowerTriangular" | custom-call | tf_op jit(solution)/shard_map/vmap(jit(_cho_solve))/triangular_solve | solution.py:29
  550.8 4.9 fusion.6
  (119 shorter events, 66.3 us)
Async XLA Ops:
  9.9 4.5 copy-start.4
  20.0 7.8 %copy-start.5 = (s32[2,16]{1,0:T(2,128)S(1)}, s32[2,16]{1,0:T(2,128)}, u32[]{:S(2)}) copy-start(s32[2,16]{1,0:T(2,128)} %param.8) | copy-start | bytes 388
  20.0 54.6 %all-to-all-start = ((f32[1024,4,128]{2,0,1:T(8,128)}), f32[1024,4,128]{2,0,1:T(8,128)S(1)}, u32[]{:S(2)}, u32[]{:S(2)}) async-start(f32[1024,4,128]{2,0,1:T(8,128)} %copy.118), calls=%async_computation | async-start | bytes 4194304 | tf_op jit(solution)/shard_map/all_to_all | solution.py:55
  26.4 114.3 %all-reduce.4.cloned.1.call-start = ((), (), s32[]{:S(2)}) async-start(), calls=%async_computation.2 | async-start | bytes 1048576 | tf_op jit(solution)/shard_map/psum | solution.py:59
  140.7 19.6 %copy-start.3 = (f32[2,256,256]{1,2,0:T(8,128)S(1)}, f32[2,256,256]{1,2,0:T(8,128)}, u32[]{:S(2)}) copy-start(f32[2,256,256]{1,2,0:T(8,128)} %all-reduce.4.cloned.1.call-done) | copy-start | bytes 1572868
  161.7 0.8 copy-start.1
  292.1 52.0 %all-to-all-start.1 = ((f32[1024,4,128]{2,0,1:T(8,128)}), f32[1024,4,128]{2,0,1:T(8,128)}, u32[]{:S(2)}, u32[]{:S(2)}) async-start(f32[1024,4,128]{2,0,1:T(8,128)} %copy.140), calls=%async_computation.1 | async-start | bytes 4194304 | tf_op jit(solution)/shard_map/all_to_all | solution.py:55
  296.7 113.5 %all-reduce.6.cloned.1.call-start = ((), (), s32[]{:S(2)}) async-start(), calls=%async_computation.3 | async-start | bytes 1048576 | tf_op jit(solution)/shard_map/psum | solution.py:59
  410.1 19.6 %copy-start.2 = (f32[2,256,256]{1,2,0:T(8,128)S(1)}, f32[2,256,256]{1,2,0:T(8,128)}, u32[]{:S(2)}) copy-start(f32[2,256,256]{1,2,0:T(8,128)} %all-reduce.6.cloned.1.call-done) | copy-start | bytes 1572868
  431.2 0.8 copy-start
Sparse Core Ops, SparseCore 0:
  87.0 53.6 all-reduce.3
  358.1 52.0 all-reduce.5
where the time goes:
time: 572 us; the launch traced here: 566 us
  other arithmetic  218 us (38%)
  waiting for transfers between devices  198 us (35%)
  local copies, waits for them, and re-layouts  72 us (13%)
  matrix products  52.7 us (9%)
  between operations  14.1 us (2%)
  starting transfers between devices  11 us (2%)
    another operation x18, other arithmetic, cayley(): lower_factor = jnp.linalg.cholesky(definite)  135 us
    psum x2, waiting for transfers between devices, on_device(): gram_matrix = lax.psum(local_gram(paired, paired), 'row')  106 us
    all_to_all x2, waiting for transfers between devices, on_device(): lax.all_to_all(outgoing, 'col', split_axis=1, concat_axis=1, tiled=True)  91.7 us
    another operation x6, other arithmetic, cayley(): return jax.scipy.linalg.cho_solve((lower_factor, True), numerator)  79.3 us
    psum x2, local copies, waits for them, and re-layouts, on_device(): gram_matrix = lax.psum(local_gram(paired, paired), 'row')  34.4 us
  transfers between devices with their start and end apart: 4, of which 4 were waited for; matrix products, arithmetic and copies ran while one was open for 1% of the time, Pallas kernels for 0%

commit v1 on v0

--- a/solution.py
+++ b/solution.py
@@ -56,7 +56,7 @@
         take_pick = (wanted[:, None] // slot_count == group_ids[None, :]).astype(jnp.float32)
         arranged = jnp.einsum("sd,rdw->rsw", take_pick, incoming, precision=precise)
         paired = arranged.reshape(rows_here, pair_count, 2 * W)
-        gram_matrix = lax.psum(local_gram(paired, paired), "row")
+        gram_matrix = jnp.sum(lax.all_gather(local_gram(paired, paired), "row"), axis=0)
         diagonal_terms = jnp.diagonal(gram_matrix, axis1=1, axis2=2)
         skew_matrix = skew_terms(gram_matrix, diagonal_terms, diagonal_terms)
         rotations = jax.vmap(cayley)(skew_matrix)

time: 572 us -> 542 us (0.948)
  waiting for transfers between devices: 198 us -> 164 us
    psum x2 -> x0, waiting for transfers between devices: 106 us -> none  [on_device(): gram_matrix = lax.psum(local_gram(paired, paired), 'row')]
    all_gather x0 -> x2, waiting for transfers between devices: none -> 70.9 us  [on_device(): lax.all_gather(local_gram(paired, paired), 'row')]
    psum x2 -> x0, local copies, waits for them, and re-layouts: 34.4 us -> none  [on_device(): gram_matrix = lax.psum(local_gram(paired, paired), 'row')]
    reduce_sum x0 -> x4, local copies, waits for them, and re-layouts: none -> 33.3 us  [on_device(): jnp.sum(lax.all_gather(local_gram(paired, paired), 'row'), axis=0)]
where the time goes in v1:
time: 542 us; the launch traced here: 537 us
  other arithmetic  223 us (41%)
  waiting for transfers between devices  164 us (30%)
  local copies, waits for them, and re-layouts  70.6 us (13%)
  matrix products  54.1 us (10%)
  between operations  14.1 us (3%)
  starting transfers between devices  11.2 us (2%)
    another operation x18, other arithmetic, cayley(): lower_factor = jnp.linalg.cholesky(definite)  135 us
    all_to_all x2, waiting for transfers between devices, on_device(): lax.all_to_all(outgoing, 'col', split_axis=1, concat_axis=1, tiled=True)  92.6 us
    another operation x6, other arithmetic, cayley(): return jax.scipy.linalg.cho_solve((lower_factor, True), numerator)  79.3 us
    all_gather x2, waiting for transfers between devices, on_device(): lax.all_gather(local_gram(paired, paired), 'row')  70.9 us
    reduce_sum x4, local copies, waits for them, and re-layouts, on_device(): jnp.sum(lax.all_gather(local_gram(paired, paired), 'row'), axis=0)  33.3 us
    all_to_all x2, starting transfers between devices, on_device(): lax.all_to_all(outgoing, 'col', split_axis=1, concat_axis=1, tiled=True)  11 us
  transfers between devices with their start and end apart: 4, of which 4 were waited for; matrix products, arithmetic and copies ran while one was open for 1% of the time, Pallas kernels for 0%

profile of v1, /device:TPU:0, one launch (start us, length us, event | category | flops | bytes accessed | tf_op | source)
XLA Modules:
  0.0 536.9 jit_solution(11085884596073870667)
XLA Ops:
  20.0 6.5 %all-to-all-start = ((f32[1024,4,128]{2,0,1:T(8,128)}), f32[1024,4,128]{2,0,1:T(8,128)S(1)}, u32[]{:S(2)}, u32[]{:S(2)}) async-start(f32[1024,4,128]{2,0,1:T(8,128)} %copy.118), calls=%async_computation | async-start | bytes 4194304 | tf_op jit(solution)/shard_map/all_to_all | solution.py:55
  29.1 45.6 %all-to-all-done = f32[1024,4,128]{2,0,1:T(8,128)S(1)} async-done(((f32[1024,4,128]{2,0,1:T(8,128)}), f32[1024,4,128]{2,0,1:T(8,128)S(1)}, u32[]{:S(2)}, u32[]{:S(2)}) %all-to-all-start) | async-done | bytes 2097184 | tf_op jit(solution)/shard_map/all_to_all | solution.py:55
  74.6 4.6 fusion.17
  82.6 4.3 fusion.12
  87.1 35.9 %all-gather.5.cloned.1.call-done = f32[16,256,256]{2,1,0:T(8,128)} async-done(((f32[2,256,256]{2,1,0:T(8,128)}), f32[16,256,256]{2,1,0:T(8,128)}) %all-gather.5.cloned.1.call-update) | async-done | bytes 4194320 | tf_op jit(solution)/shard_map/all_gather | solution.py:59
  125.5 16.5 %copy.122 = f32[2,256,256]{0,2,1:T(8,128)} copy(f32[2,256,256]{2,1,0:T(8,128)S(1)} %reduce_sum.18) | data formatting | bytes 1048576 | tf_op jit(solution)/shard_map/reduce_sum | solution.py:59
  149.0 24.0 %custom-call.23 = f32[2,128,128]{2,1,0:T(8,128)S(1)} custom-call(f32[2,128,128]{2,1,0:T(8,128)S(1)} %cholesky.198), custom_call_target="Cholesky" | custom-call | tf_op jit(solution)/shard_map/vmap(jit(cholesky))/cholesky | solution.py:28
  173.1 19.7 %custom-call.24 = f32[2,1,128,128]{2,3,1,0:T(8,128)S(1)} custom-call(f32[2,1,128,128]{3,2,1,0:T(8,128)S(1)} %select_bitcast_fusion.1), custom_call_target="InvertDiagBlocksLowerTriangular" | custom-call | tf_op jit(solution)/shard_map/vmap(jit(cholesky))/cholesky | solution.py:28
  195.3 23.5 %custom-call.25 = f32[2,128,128]{2,1,0:T(8,128)S(1)} custom-call(f32[2,128,128]{2,1,0:T(8,128)S(1)} %convolution_subtract_fusion.5), custom_call_target="Cholesky" | custom-call | tf_op jit(solution)/shard_map/vmap(jit(cholesky))/cholesky | solution.py:28
  219.3 4.1 while.4
  223.4 39.5 %custom-call.26 = f32[2,2,128,128]{2,3,1,0:T(8,128)S(1)} custom-call(f32[2,2,128,128]{3,2,1,0:T(8,128)S(1)} %bitcast.147), custom_call_target="InvertDiagBlocksLowerTriangular" | custom-call | tf_op jit(solution)/shard_map/vmap(jit(_cho_solve))/triangular_solve | solution.py:29
  267.2 4.8 fusion.10
  277.8 4.6 all-to-all-start.1
  283.9 47.1 %all-to-all-done.1 = f32[1024,4,128]{2,0,1:T(8,128)S(1)} async-done(((f32[1024,4,128]{2,0,1:T(8,128)}), f32[1024,4,128]{2,0,1:T(8,128)S(1)}, u32[]{:S(2)}, u32[]{:S(2)}) %all-to-all-start.1) | async-done | bytes 2097184 | tf_op jit(solution)/shard_map/all_to_all | solution.py:55
  331.0 4.6 fusion.20
  338.7 4.3 fusion.8
  343.0 35.0 %all-gather.7.cloned.1.call-done = f32[16,256,256]{2,1,0:T(8,128)} async-done(((f32[2,256,256]{2,1,0:T(8,128)}), f32[16,256,256]{2,1,0:T(8,128)}) %all-gather.7.cloned.1.call-update) | async-done | bytes 4194320 | tf_op jit(solution)/shard_map/all_gather | solution.py:59
  380.6 16.5 %copy.146 = f32[2,256,256]{0,2,1:T(8,128)} copy(f32[2,256,256]{2,1,0:T(8,128)S(1)} %reduce_sum.19) | data formatting | bytes 1048576 | tf_op jit(solution)/shard_map/reduce_sum | solution.py:59
  404.1 23.9 %custom-call.27 = f32[2,128,128]{2,1,0:T(8,128)S(1)} custom-call(f32[2,128,128]{2,1,0:T(8,128)S(1)} %cholesky.201), custom_call_target="Cholesky" | custom-call | tf_op jit(solution)/shard_map/vmap(jit(cholesky))/cholesky | solution.py:28
  428.1 19.7 %custom-call.28 = f32[2,1,128,128]{2,3,1,0:T(8,128)S(1)} custom-call(f32[2,1,128,128]{3,2,1,0:T(8,128)S(1)} %select_bitcast_fusion), custom_call_target="InvertDiagBlocksLowerTriangular" | custom-call | tf_op jit(solution)/shard_map/vmap(jit(cholesky))/cholesky | solution.py:28
  450.3 23.5 %custom-call.29 = f32[2,128,128]{2,1,0:T(8,128)S(1)} custom-call(f32[2,128,128]{2,1,0:T(8,128)S(1)} %convolution_subtract_fusion.4), custom_call_target="Cholesky" | custom-call | tf_op jit(solution)/shard_map/vmap(jit(cholesky))/cholesky | solution.py:28
  474.2 4.1 while.5
  478.3 39.5 %custom-call.30 = f32[2,2,128,128]{2,3,1,0:T(8,128)S(1)} custom-call(f32[2,2,128,128]{3,2,1,0:T(8,128)S(1)} %bitcast.146), custom_call_target="InvertDiagBlocksLowerTriangular" | custom-call | tf_op jit(solution)/shard_map/vmap(jit(_cho_solve))/triangular_solve | solution.py:29
  522.1 4.9 fusion.6
  (119 shorter events, 74.6 us)
Async XLA Ops:
  9.9 4.5 copy-start.2
  20.0 7.8 %copy-start.3 = (s32[2,16]{1,0:T(2,128)S(1)}, s32[2,16]{1,0:T(2,128)}, u32[]{:S(2)}) copy-start(s32[2,16]{1,0:T(2,128)} %param.8) | copy-start | bytes 388
  20.0 54.6 %all-to-all-start = ((f32[1024,4,128]{2,0,1:T(8,128)}), f32[1024,4,128]{2,0,1:T(8,128)S(1)}, u32[]{:S(2)}, u32[]{:S(2)}) async-start(f32[1024,4,128]{2,0,1:T(8,128)} %copy.118), calls=%async_computation | async-start | bytes 4194304 | tf_op jit(solution)/shard_map/all_to_all | solution.py:55
  26.4 96.5 %all-gather.5.cloned.1.call-start = ((), (), s32[]{:S(2)}) async-start(), calls=%async_computation.2 | async-start | bytes 4718592 | tf_op jit(solution)/shard_map/all_gather | solution.py:59
  148.2 0.8 copy-start.1
  277.8 53.2 %all-to-all-start.1 = ((f32[1024,4,128]{2,0,1:T(8,128)}), f32[1024,4,128]{2,0,1:T(8,128)S(1)}, u32[]{:S(2)}, u32[]{:S(2)}) async-start(f32[1024,4,128]{2,0,1:T(8,128)} %copy.142), calls=%async_computation.1 | async-start | bytes 4194304 | tf_op jit(solution)/shard_map/all_to_all | solution.py:55
  282.4 95.7 %all-gather.7.cloned.1.call-start = ((), (), s32[]{:S(2)}) async-start(), calls=%async_computation.3 | async-start | bytes 4718592 | tf_op jit(solution)/shard_map/all_gather | solution.py:59
  403.3 0.8 copy-start
Sparse Core Ops, SparseCore 0:
  87.1 35.8 all-gather.4
  343.2 34.8 all-gather.6
